TPU v7x, 256 devices: a whole 4x4x8 slice. The times are simulated.
256 devices in a mesh: seq: 32 (over z, y), head: 8 (over x, core).
Axes of the slice: x: 4, y: 4, z: 8, core: 2. Of those that a mesh axis runs over, the one named last changes fastest.
Arguments:
- query: bfloat16 [49152, 3072], P(('seq', 'head')), may hold values from -40 to 40
- key: bfloat16 [49152, 3072], P(('seq', 'head')), may hold values from -4 to 4
- value: bfloat16 [49152, 3072], P(('seq', 'head')), may hold values from -6 to 6
- raster_to_tile: int32 [49152], P(('seq', 'head')), may hold values from 0 to 49151, as said below
- window_list: int32 [128, 4], P('seq'), may hold values from 0 to 127, as said below
- valid_count: int32 [128], replicated, may hold values from 96 to 384
Outputs:
- attended: bfloat16 [49152, 3072], P(('seq', 'head'))
Inputs may be any that keep to these rules, and one draw needn't show every extreme that they name: `raster_to_tile`: A permutation of the slots. Raster shard d (rows d * 1536 // 8 onward, d counting seq+head) holds exactly 6 slots of every owner o, where owner o holds slots o * 1536 to (o+1) * 1536 - 1. `window_list`: row t holds t first, then 4 - 1 distinct other tiles, each within 3 tiles of t.
All inputs are finite; a program needn't handle non-finite values.
Results may differ from a plain program's by a relative error of at most 0.0036.
Values may be sent and summed in bfloat16 or wider, within the bound.
A program may use at most 64 MiB of HBM per device.

v0:
```python
import jax
import jax.numpy as jnp
from jax import lax
from jax.sharding import PartitionSpec as P

HEAD_DIM = 128


def body(query, key, value, raster_to_tile, window_list, valid_count):
    seq_count = lax.axis_size("seq")
    head_count = lax.axis_size("head")
    seq_pos = lax.axis_index("seq")
    rows_here, width = query.shape
    part_width = width // head_count
    tile_dev, win = window_list.shape
    tok_dev = rows_here * head_count
    tile = tok_dev // tile_dev
    share = rows_here // seq_count
    reach = win - 1
    rim = reach * tile
    ext_rows = tok_dev + 2 * rim
    ext_tiles = tile_dev + 2 * reach
    heads_here = part_width // HEAD_DIM
    all_tiles = valid_count.shape[0]
    order = jnp.argsort(raster_to_tile)
    slots_sorted = raster_to_tile[order].reshape(seq_count, share)
    query_sorted = query[order].reshape(seq_count, share, head_count, part_width)
    joined = jnp.concatenate(
        [
            key.reshape(rows_here, head_count, part_width),
            value.reshape(rows_here, head_count, part_width),
        ],
        axis=2,
    )
    pair_sorted = joined[order].reshape(seq_count, share, head_count, 2 * part_width)
    zero_pair = jnp.zeros_like(pair_sorted[:1])
    wide_pair = jnp.concatenate(
        [
            jnp.concatenate([zero_pair, pair_sorted[:-1]], axis=0),
            pair_sorted,
            jnp.concatenate([pair_sorted[1:], zero_pair], axis=0),
        ],
        axis=1,
    )
    empty_slots = jnp.full((1, share), -1, jnp.int32)
    wide_slots = jnp.concatenate(
        [
            jnp.concatenate([empty_slots, slots_sorted[:-1]], axis=0),
            slots_sorted,
            jnp.concatenate([slots_sorted[1:], empty_slots], axis=0),
        ],
        axis=1,
    )
    slot_send = jnp.broadcast_to(wide_slots[:, :, None], (seq_count, 3 * share, head_count))
    query_in, pair_in, slot_in = (
        lax.all_to_all(
            lax.all_to_all(query_sorted, "seq", split_axis=0, concat_axis=0, tiled=True),
            "head",
            split_axis=2,
            concat_axis=1,
            tiled=True,
        ),
        lax.all_to_all(
            lax.all_to_all(wide_pair, "seq", split_axis=0, concat_axis=0, tiled=True),
            "head",
            split_axis=2,
            concat_axis=1,
            tiled=True,
        ),
        lax.all_to_all(
            lax.all_to_all(slot_send, "seq", split_axis=0, concat_axis=0, tiled=True),
            "head",
            split_axis=2,
            concat_axis=1,
            tiled=True,
        ),
    )
    middle = slot_in.reshape(seq_count, head_count, 3, share)[:, :, 1, :]
    local = middle.reshape(tok_dev) - seq_pos * tok_dev
    place = jnp.zeros((tok_dev,), jnp.int32).at[local].set(jnp.arange(tok_dev, dtype=jnp.int32))
    query_tile = query_in.reshape(tok_dev, part_width)[place]
    every_slot = slot_in.reshape(3 * tok_dev)
    shifted = every_slot - (seq_pos * tok_dev - rim)
    target = jnp.where((every_slot >= 0) & (shifted >= 0) & (shifted < ext_rows), shifted, ext_rows)
    place_ext = (
        jnp.full((ext_rows,), 3 * tok_dev, jnp.int32)
        .at[target]
        .set(jnp.arange(3 * tok_dev, dtype=jnp.int32), mode="drop")
    )
    padded = jnp.concatenate(
        [
            pair_in.reshape(3 * tok_dev, 2 * part_width),
            jnp.zeros((1, 2 * part_width), pair_in.dtype),
        ],
        axis=0,
    )
    pair_ext = padded[place_ext]
    first_tile = seq_pos * tile_dev - reach
    global_tiles = jnp.clip(first_tile + jnp.arange(ext_tiles, dtype=jnp.int32), 0, all_tiles - 1)
    key_usable = jnp.arange(tile, dtype=jnp.int32)[None, :] < valid_count[global_tiles][:, None]
    own_usable = key_usable[reach : reach + tile_dev]
    local_windows = window_list - first_tile
    query_blocks = query_tile.reshape(tile_dev, tile, heads_here, HEAD_DIM)
    pair_blocks = pair_ext.reshape(ext_tiles, tile, 2, heads_here, HEAD_DIM)
    scale = HEAD_DIM ** (-0.5)

    def one_tile(item):
        query_blk, windows, query_usable = item
        picked = pair_blocks[windows]
        keys_blk = picked[:, :, 0].reshape(win * tile, heads_here, HEAD_DIM)
        values_blk = picked[:, :, 1].reshape(win * tile, heads_here, HEAD_DIM)
        usable = key_usable[windows].reshape(win * tile)
        scores = (
            jnp.einsum("qhd,khd->hqk", query_blk, keys_blk, preferred_element_type=jnp.float32)
            * scale
        )
        scores = jnp.where(usable[None, None, :], scores, -jnp.inf)
        top = jnp.max(scores, axis=2, keepdims=True)
        weights = jnp.exp(scores - top)
        total = jnp.sum(weights, axis=2)
        mixed = jnp.einsum(
            "hqk,khd->qhd",
            weights.astype(jnp.bfloat16),
            values_blk,
            preferred_element_type=jnp.float32,
        )
        mixed = mixed / jnp.transpose(total)[:, :, None]
        mixed = jnp.where(query_usable[:, None, None], mixed, 0.0)
        return mixed.astype(jnp.bfloat16).reshape(tile, part_width)

    out_tile = lax.map(one_tile, (query_blocks, local_windows, own_usable)).reshape(
        tok_dev, part_width
    )
    outgoing = out_tile[local].reshape(seq_count, head_count, share, 1, part_width)
    arrived = lax.all_to_all(
        lax.all_to_all(outgoing, "seq", split_axis=0, concat_axis=0, tiled=True),
        "head",
        split_axis=1,
        concat_axis=3,
        tiled=True,
    )
    sorted_rows = arrived.reshape(rows_here, width)
    inverse = (
        jnp.zeros((rows_here,), jnp.int32).at[order].set(jnp.arange(rows_here, dtype=jnp.int32))
    )
    return sorted_rows[inverse]


def solution(mesh):
    placed = (
        P(("seq", "head"), None),
        P(("seq", "head"), None),
        P(("seq", "head"), None),
        P(("seq", "head")),
        P("seq", None),
        P(),
    )
    return jax.shard_map(
        body, mesh=mesh, in_specs=placed, out_specs=P(("seq", "head"), None), check_vma=False
    )
```

profile of v0, /device:TPU:1, one launch (start us, length us, event | category | flops | bytes accessed | tf_op | source)
XLA Modules:
  0.0 554.6 jit_solution(8304889225877488797)
XLA Ops:
  0.0 3.9 sort.17
  4.0 2.0 gather_fusion.4
  6.6 20.5 %all_to_all.80 = s32[32,1,144]{2,1,0:T(1,128)S(1)} all-to-all(s32[32,1,144]{2,1,0:T(1,128)S(1)} %reshape.329), channel_id=1, replica_groups=mesh['seq'=32,'head'=8] {'seq'}, dimensions={0} | all-to-all | bytes 36864 | tf_op jit(solution)/shard_map/all_to_all | solution.py:71
  27.7 0.8 reduce.6
  28.7 0.7 reshape.331
  29.4 6.4 %all-to-all-start.3 = ((s32[8,1,576]{2,1,0:T(1,128)}), s32[8,1,576]{2,1,0:T(1,128)}, u32[]{:S(2)}, u32[]{:S(2)}) async-start(s32[8,1,576]{2,1,0:T(1,128)} %reshape.331), calls=%async_computation.3 | async-start | bytes 40960 | tf_op jit(solution)/shard_map/all_to_all | solution.py:70
  35.8 1.3 gather_fusion.6
  37.1 1.2 copy.69
  38.4 2.2 all-to-all-done.3
  40.6 4.1 all-to-all-start.4
  45.1 1.6 pad_maximum_fusion
  46.7 2.5 gather_fusion.3
  49.6 3.3 fusion.37
  52.9 21.1 %all-to-all-done.4 = bf16[32,6,8,384]{3,2,1,0:T(8,128)(2,1)S(1)} async-done(((bf16[32,6,8,384]{3,2,1,0:T(8,128)(2,1)}), bf16[32,6,8,384]{3,2,1,0:T(8,128)(2,1)S(1)}, u32[]{:S(2)}, u32[]{:S(2)}) %all-to-all-start.4) | async-done | bytes 1179680 | tf_op jit(solution)/shard_map/all_to_all | solution.py:57
  74.0 6.5 %all-to-all-start = ((bf16[32,18,8,768]{3,2,1,0:T(8,128)(2,1)}), bf16[32,18,8,768]{3,2,1,0:T(8,128)(2,1)}, u32[]{:S(2)}, u32[]{:S(2)}) async-start(bf16[32,18,8,768]{3,2,1,0:T(8,128)(2,1)} %fusion.37), calls=%async_computation | async-start | bytes 14155776 | tf_op jit(solution)/shard_map/all_to_all | solution.py:64
  80.5 1.3 copy.50
  81.8 152.8 %all-to-all-done = bf16[32,18,8,768]{3,2,1,0:T(8,128)(2,1)} async-done(((bf16[32,18,8,768]{3,2,1,0:T(8,128)(2,1)}), bf16[32,18,8,768]{3,2,1,0:T(8,128)(2,1)}, u32[]{:S(2)}, u32[]{:S(2)}) %all-to-all-start) | async-done | bytes 7077920 | tf_op jit(solution)/shard_map/all_to_all | solution.py:64
  234.5 9.1 %all-to-all-start.5 = ((bf16[32,6,8,384]{3,0,1,2:T(8,128)(2,1)}), bf16[32,6,8,384]{3,0,1,2:T(8,128)(2,1)S(1)}, u32[]{:S(2)}, u32[]{:S(2)}) async-start(bf16[32,6,8,384]{3,0,1,2:T(8,128)(2,1)} %copy.50), calls=%async_computation.5 | async-start | bytes 2359296 | tf_op jit(solution)/shard_map/all_to_all | solution.py:56
  243.7 8.3 %copy.44 = bf16[32,18,8,768]{3,0,1,2:T(8,128)(2,1)} copy(bf16[32,18,8,768]{3,2,1,0:T(8,128)(2,1)} %all-to-all-done) | data formatting | bytes 14155776 | tf_op jit(solution)/shard_map/all_to_all | solution.py:64
  252.0 8.2 %all-to-all-done.5 = bf16[32,6,8,384]{3,0,1,2:T(8,128)(2,1)S(1)} async-done(((bf16[32,6,8,384]{3,0,1,2:T(8,128)(2,1)}), bf16[32,6,8,384]{3,0,1,2:T(8,128)(2,1)S(1)}, u32[]{:S(2)}, u32[]{:S(2)}) %all-to-all-start.5) | async-done | bytes 1179680 | tf_op jit(solution)/shard_map/all_to_all | solution.py:56
  260.2 5.6 %all-to-all-start.1 = ((bf16[32,18,8,768]{3,0,1,2:T(8,128)(2,1)}), bf16[32,18,8,768]{3,0,1,2:T(8,128)(2,1)}, u32[]{:S(2)}, u32[]{:S(2)}) async-start(bf16[32,18,8,768]{3,0,1,2:T(8,128)(2,1)} %copy.44), calls=%async_computation.1 | async-start | bytes 14155776 | tf_op jit(solution)/shard_map/all_to_all | solution.py:63
  266.6 1.5 reduce.7
  269.2 6.2 %scatter_custom_fusion.1 = s32[1536]{0:T(1024)S(1)} fusion(s32[1536]{0:T(1024)S(1)} %fusion.42, s32[1536]{0:T(1024)S(1)} %iota.24, s32[]{:T(128)} %constant.29.clone.1), kind=kCustom, calls=%fused_computation.70 | custom fusion | bytes 6148 | tf_op jit(solution)/shard_map/scatter | solution.py:80
  275.5 17.6 %scatter_custom_fusion = s32[3840]{0:T(1024)S(1)} fusion(s32[4608]{0:T(1024)S(1)} %fusion.39, s32[4608]{0:T(1024)S(1)} %iota.23, s32[]{:T(128)} %constant.14.clone.1), kind=kCustom, calls=%fused_computation.63 | custom fusion | bytes 15364 | tf_op jit(solution)/shard_map/scatter | solution.py:88
  293.2 1.6 copy.51
  294.8 2.3 reshape.197
  297.1 5.3 gather_fusion.7
  302.4 3.3 reshape.319
  305.7 1.3 copy.54
  307.0 38.6 %all-to-all-done.1 = bf16[32,18,8,768]{3,0,1,2:T(8,128)(2,1)} async-done(((bf16[32,18,8,768]{3,0,1,2:T(8,128)(2,1)}), bf16[32,18,8,768]{3,0,1,2:T(8,128)(2,1)}, u32[]{:S(2)}, u32[]{:S(2)}) %all-to-all-start.1) | async-done | bytes 7077920 | tf_op jit(solution)/shard_map/all_to_all | solution.py:63
  345.6 10.9 %copy.45 = bf16[32,8,18,1,768]{4,2,1,0,3:T(8,128)(2,1)} copy(bf16[32,8,18,1,768]{4,0,2,1,3:T(8,128)(2,1)} %bitcast.5) | data formatting | bytes 14155776 | tf_op jit(solution)/shard_map/all_to_all | solution.py:63
  356.5 11.5 %reshape.193 = bf16[4608,768]{1,0:T(8,128)(2,1)} reshape(bf16[32,8,18,1,768]{4,2,1,0,3:T(8,128)(2,1)} %copy.45) | data formatting | bytes 14155776 | tf_op jit(solution)/shard_map/reshape | solution.py:92
  368.0 6.4 %concatenate.28 = bf16[4609,768]{1,0:T(8,128)(2,1)} pad(bf16[4608,768]{1,0:T(8,128)(2,1)} %reshape.193, bf16[]{:T(256)} %constant.30.clone.1), padding=0_1x0_0 | pad | bytes 14157314 | tf_op jit(solution)/shard_map/concatenate | solution.py:90
  374.3 18.8 %gather_fusion.5 = bf16[3840,768]{1,0:T(8,128)(2,1)} fusion(bf16[4609,768]{1,0:T(8,128)(2,1)} %concatenate.28, s32[4096]{0:T(1024)S(1)} %pad_clamp_fusion.1), kind=kCustom, calls=%fused_computation.5 | custom fusion | bytes 11811840 | tf_op jit(solution)/shard_map/gather | solution.py:97
  393.1 13.8 %reshape.195 = bf16[10,384,2,3,128]{4,3,2,1,0:T(4,128)(2,1)} reshape(bf16[3840,768]{1,0:T(8,128)(2,1)} %gather_fusion.5) | data formatting | bytes 11796480 | tf_op jit(solution)/shard_map/reshape | solution.py:104
  406.9 71.9 %while.11 = (s32[]{:T(128)}, bf16[4,384,384]{2,1,0:T(8,128)(2,1)S(1)}, pred[4,384]{1,0:T(4,128)(4,1)S(1)}, s32[4,4]{1,0:T(4,128)S(1)}, bf16[10,384,2,3,128]{4,3,...) while((s32[]{:T(128)}, ...), condition=%wide.region_6.7_spmd.clone, body=%wide.region_3.6_spmd.clone.sunk | while | flops 925878784 | bytes 37202520 | solution.py:131
  407.6 8.1 %gather_fusion.1 = bf16[4,384,2,3,128]{4,3,2,1,0:T(4,128)(2,1)} fusion(bf16[10,384,2,3,128]{4,3,2,1,0:T(4,128)(2,1)} %get-tuple-element.185, s32[1024]{0:T(1024)S(1)} %pad_clamp_fusion.8), kind=kCustom, calls=%fused_computation.clone.clone.1 | custom fusion | bytes 4718608 | tf_op jit(solution)/shard_map/while/body/eval_jaxpr/gather | solution.py:109
  415.6 3.0 fusion.64
  418.8 2.2 fusion.65
  421.0 1.5 fusion.66
  422.5 2.0 fusion.67
  425.6 8.1 %gather_fusion.1 = bf16[4,384,2,3,128]{4,3,2,1,0:T(4,128)(2,1)} fusion(bf16[10,384,2,3,128]{4,3,2,1,0:T(4,128)(2,1)} %get-tuple-element.185, s32[1024]{0:T(1024)S(1)} %pad_clamp_fusion.8), kind=kCustom, calls=%fused_computation.clone.clone.1 | custom fusion | bytes 4718608 | tf_op jit(solution)/shard_map/while/body/eval_jaxpr/gather | solution.py:109
  433.6 3.0 fusion.64
  436.8 2.2 fusion.65
  439.0 1.5 fusion.66
  440.5 2.0 fusion.67
  443.6 8.1 %gather_fusion.1 = bf16[4,384,2,3,128]{4,3,2,1,0:T(4,128)(2,1)} fusion(bf16[10,384,2,3,128]{4,3,2,1,0:T(4,128)(2,1)} %get-tuple-element.185, s32[1024]{0:T(1024)S(1)} %pad_clamp_fusion.8), kind=kCustom, calls=%fused_computation.clone.clone.1 | custom fusion | bytes 4718608 | tf_op jit(solution)/shard_map/while/body/eval_jaxpr/gather | solution.py:109
  451.6 3.0 fusion.64
  454.8 2.2 fusion.65
  457.0 1.5 fusion.66
  458.5 2.0 fusion.67
  461.5 8.1 %gather_fusion.1 = bf16[4,384,2,3,128]{4,3,2,1,0:T(4,128)(2,1)} fusion(bf16[10,384,2,3,128]{4,3,2,1,0:T(4,128)(2,1)} %get-tuple-element.185, s32[1024]{0:T(1024)S(1)} %pad_clamp_fusion.8), kind=kCustom, calls=%fused_computation.clone.clone.1 | custom fusion | bytes 4718608 | tf_op jit(solution)/shard_map/while/body/eval_jaxpr/gather | solution.py:109
  469.6 3.0 fusion.64
  472.8 2.2 fusion.65
  475.0 1.5 fusion.66
  476.5 2.0 fusion.67
  478.8 5.3 gather_fusion.8
  484.1 2.2 reshape.201
  486.6 40.7 %all_to_all.81 = bf16[32,8,6,1,384]{4,1,3,2,0:T(8,128)(2,1)S(1)} all-to-all(bf16[32,8,6,1,384]{4,1,3,2,0:T(8,128)(2,1)S(1)} %copy.56), channel_id=1, replica_groups=mesh['seq'=32,'head'=8] {'seq'}, dimensions={0} | all-to-all | bytes 2359296 | tf_op jit(solution)/shard_map/all_to_all | solution.py:136
  527.3 1.3 copy.57
  528.6 6.3 %all-to-all-start.7 = ((bf16[32,8,6,1,384]{4,0,3,2,1:T(8,128)(2,1)}), bf16[32,8,6,1,384]{4,0,3,2,1:T(8,128)(2,1)S(1)}, u32[]{:S(2)}, u32[]{:S(2)}) async-start(bf16[32,8,6,1,384]{4,0,3,2,1:T(8,128)(2,1)} %copy.57), calls=%async_computation.7 | async-start | bytes 2359296 | tf_op jit(solution)/shard_map/all_to_all | solution.py:135
  534.9 1.2 scatter_custom_fusion.2
  536.1 15.3 %all-to-all-done.7 = bf16[32,8,6,1,384]{4,0,3,2,1:T(8,128)(2,1)S(1)} async-done(((bf16[32,8,6,1,384]{4,0,3,2,1:T(8,128)(2,1)}), bf16[32,8,6,1,384]{4,0,3,2,1:T(8,128)(2,1)S(1)}, u32[]{:S(2)}, u32[]{:S(2)}) %all-to-all-start.7) | async-done | bytes 1179680 | tf_op jit(solution)/shard_map/all_to_all | solution.py:135
  552.3 2.3 gather_fusion.9
  (96 shorter events, 10.1 us)
Async XLA Ops:
  0.0 35.8 %copy-start = (bf16[192,3072]{1,0:T(8,128)(2,1)S(1)}, bf16[192,3072]{1,0:T(8,128)(2,1)}, u32[]{:S(2)}) copy-start(bf16[192,3072]{1,0:T(8,128)(2,1)} %param.8) | copy-start | bytes 3538948
  29.4 11.2 %all-to-all-start.3 = ((s32[8,1,576]{2,1,0:T(1,128)}), s32[8,1,576]{2,1,0:T(1,128)}, u32[]{:S(2)}, u32[]{:S(2)}) async-start(s32[8,1,576]{2,1,0:T(1,128)} %reshape.331), calls=%async_computation.3 | async-start | bytes 40960 | tf_op jit(solution)/shard_map/all_to_all | solution.py:70
  37.1 7.6 %copy-start.3 = (bf16[192,3072]{1,0:T(8,128)(2,1)S(1)}, bf16[192,3072]{1,0:T(8,128)(2,1)}, u32[]{:S(2)}) copy-start(bf16[192,3072]{1,0:T(8,128)(2,1)} %param.9) | copy-start | bytes 3538948
  40.6 4.3 copy-start.4
  40.6 33.4 %all-to-all-start.4 = ((bf16[32,6,8,384]{3,2,1,0:T(8,128)(2,1)}), bf16[32,6,8,384]{3,2,1,0:T(8,128)(2,1)S(1)}, u32[]{:S(2)}, u32[]{:S(2)}) async-start(bf16[32,6,8,384]{3,2,1,0:T(8,128)(2,1)} %bitcast.38), calls=%async_computation.4 | async-start | bytes 2359296 | tf_op jit(solution)/shard_map/all_to_all | solution.py:57
  74.0 160.5 %all-to-all-start = ((bf16[32,18,8,768]{3,2,1,0:T(8,128)(2,1)}), bf16[32,18,8,768]{3,2,1,0:T(8,128)(2,1)}, u32[]{:S(2)}, u32[]{:S(2)}) async-start(bf16[32,18,8,768]{3,2,1,0:T(8,128)(2,1)} %fusion.37), calls=%async_computation | async-start | bytes 14155776 | tf_op jit(solution)/shard_map/all_to_all | solution.py:64
  234.5 25.7 %all-to-all-start.5 = ((bf16[32,6,8,384]{3,0,1,2:T(8,128)(2,1)}), bf16[32,6,8,384]{3,0,1,2:T(8,128)(2,1)S(1)}, u32[]{:S(2)}, u32[]{:S(2)}) async-start(bf16[32,6,8,384]{3,0,1,2:T(8,128)(2,1)} %copy.50), calls=%async_computation.5 | async-start | bytes 2359296 | tf_op jit(solution)/shard_map/all_to_all | solution.py:56
  252.0 13.8 %copy-start.2 = (s32[128]{0:T(128)S(1)}, s32[128]{0:T(128)}, u32[]{:S(2)}) copy-start(s32[128]{0:T(128)} %param.13) | copy-start | bytes 1540
  252.0 14.6 %copy-start.5 = (s32[4,4]{1,0:T(4,128)S(1)}, s32[4,4]{1,0:T(4,128)}, u32[]{:S(2)}) copy-start(s32[4,4]{1,0:T(4,128)} %param.12) | copy-start | bytes 196
  260.2 85.4 %all-to-all-start.1 = ((bf16[32,18,8,768]{3,0,1,2:T(8,128)(2,1)}), bf16[32,18,8,768]{3,0,1,2:T(8,128)(2,1)}, u32[]{:S(2)}, u32[]{:S(2)}) async-start(bf16[32,18,8,768]{3,0,1,2:T(8,128)(2,1)} %copy.44), calls=%async_computation.1 | async-start | bytes 14155776 | tf_op jit(solution)/shard_map/all_to_all | solution.py:63
  528.6 22.8 %all-to-all-start.7 = ((bf16[32,8,6,1,384]{4,0,3,2,1:T(8,128)(2,1)}), bf16[32,8,6,1,384]{4,0,3,2,1:T(8,128)(2,1)S(1)}, u32[]{:S(2)}, u32[]{:S(2)}) async-start(bf16[32,8,6,1,384]{4,0,3,2,1:T(8,128)(2,1)} %copy.57), calls=%async_computation.7 | async-start | bytes 2359296 | tf_op jit(solution)/shard_map/all_to_all | solution.py:135
  552.3 2.3 copy-start.1
where the time goes:
time: 557 us; the launch traced here: 555 us
  waiting for transfers between devices  238 us (43%)
  local copies, waits for them, and re-layouts  182 us (33%)
  blocking collectives  61.3 us (11%)
  starting transfers between devices  37.9 us (7%)
  other arithmetic  17.9 us (3%)
  matrix products  16.8 us (3%)
    all_to_all x1, waiting for transfers between devices, body(): lax.all_to_all(wide_pair, 'seq', split_axis=0, concat_axis=0, tiled=True)  153 us
    all_to_all x1, blocking collectives, body(): lax.all_to_all(outgoing, 'seq', split_axis=0, concat_axis=0, tiled=True)  40.7 us
    all_to_all x1, waiting for transfers between devices, body(): lax.all_to_all(lax.all_to_all(wide_pair, 'seq', split_axis=0, concat_axis...  38.6 us
    gather x4, local copies, waits for them, and re-layouts, one_tile(): picked = pair_blocks[windows]  32.2 us
    all_to_all x1, waiting for transfers between devices, body(): lax.all_to_all(query_sorted, 'seq', split_axis=0, concat_axis=0, tiled=True)  21.1 us
    all_to_all x1, blocking collectives, body(): lax.all_to_all(slot_send, 'seq', split_axis=0, concat_axis=0, tiled=True)  20.5 us
    gather x1, local copies, waits for them, and re-layouts, body(): pair_ext = padded[place_ext]  18.8 us
    scatter x1, local copies, waits for them, and re-layouts, body(): place_ext = jnp.full((ext_rows,), 3 * tok_dev, jnp.int32).at[target].set(...  17.6 us
  transfers between devices with their start and end apart: 6, of which 6 were waited for; matrix products, arithmetic and copies ran while one was open for 11% of the time, Pallas kernels for 0%

commit v1 on v0

--- a/solution.py
+++ b/solution.py
@@ -4,6 +4,29 @@
 from jax.sharding import PartitionSpec as P
 
 HEAD_DIM = 128
+
+
+def cut_along(value, dim, length):
+    dims = value.shape
+    parts = value.reshape(*dims[:dim], length, dims[dim] // length, *dims[dim + 1 :])
+    return jnp.moveaxis(parts, dim, 0)
+
+
+def laid_out(blocks, dim):
+    shape = list(blocks.shape[1:])
+    shape[dim] *= blocks.shape[0]
+    return jnp.moveaxis(blocks, 0, dim).reshape(shape)
+
+
+def swapped_with_each(shard, axis, split_dim, concat_dim):
+    size, place = (lax.axis_size(axis), lax.axis_index(axis))
+    blocks = cut_along(shard, split_dim, size)
+    outs = [blocks[place]]
+    for hop in range(1, size):
+        sent = blocks[place ^ hop]
+        outs.append(lax.ppermute(sent, axis, [(i, i ^ hop) for i in range(size)]))
+    blocks = jnp.stack(outs)[place ^ jnp.arange(size)]
+    return laid_out(blocks, concat_dim)
 
 
 def body(query, key, value, raster_to_tile, window_list, valid_count):
@@ -67,12 +90,8 @@
             concat_axis=1,
             tiled=True,
         ),
-        lax.all_to_all(
-            lax.all_to_all(slot_send, "seq", split_axis=0, concat_axis=0, tiled=True),
-            "head",
-            split_axis=2,
-            concat_axis=1,
-            tiled=True,
+        swapped_with_each(
+            lax.all_to_all(slot_send, "seq", split_axis=0, concat_axis=0, tiled=True), "head", 2, 1
         ),
     )
     middle = slot_in.reshape(seq_count, head_count, 3, share)[:, :, 1, :]

time: 557 us -> 588 us (1.056); the launches traced: 555 us -> 578 us
  waiting for transfers between devices: 238 us -> 252 us
  starting transfers between devices: 37.9 us -> 47.9 us
    ppermute x0 -> x7, waiting for transfers between devices: none -> 66.6 us  [swapped_with_each(): outs.append(lax.ppermute(sent, axis, [(i, i ^ hop) for i in range(size)]))]
    all_to_all x1, waiting for transfers between devices: 38.6 us -> 0.01 us  [body(): lax.all_to_all(lax.all_to_all(wide_pair, 'seq', split_axis=0, concat_axis...]
    all_to_all x2 -> x1, waiting for transfers between devices: 17.5 us -> 5.93 us  [body(): lax.all_to_all(slot_send, 'seq', split_axis=0, concat_axis=0, tiled=True)]
    ppermute x0 -> x7, starting transfers between devices: none -> 11.4 us  [swapped_with_each(): outs.append(lax.ppermute(sent, axis, [(i, i ^ hop) for i in range(size)]))]
    all_to_all x2 -> x1, starting transfers between devices: 12.7 us -> 12.2 us  [body(): lax.all_to_all(slot_send, 'seq', split_axis=0, concat_axis=0, tiled=True)]
  transfers between devices with their start and end apart: 6 -> 12, of which waited for: 6 -> 6; matrix products, arithmetic and copies ran while one was open for 11% -> 11% of each run, Pallas kernels for 0% -> 0%
where the time goes in v1:
time: 588 us; the launch traced here: 578 us
  waiting for transfers between devices  252 us (43%)
  local copies, waits for them, and re-layouts  182 us (31%)
  blocking collectives  61.3 us (10%)
  starting transfers between devices  47.9 us (8%)
  other arithmetic  17.2 us (3%)
  matrix products  16.7 us (3%)
    all_to_all x1, waiting for transfers between devices, body(): lax.all_to_all(wide_pair, 'seq', split_axis=0, concat_axis=0, tiled=True)  151 us
    ppermute x7, waiting for transfers between devices, swapped_with_each(): outs.append(lax.ppermute(sent, axis, [(i, i ^ hop) for i in range(size)]))  66.6 us
    all_to_all x1, blocking collectives, body(): lax.all_to_all(outgoing, 'seq', split_axis=0, concat_axis=0, tiled=True)  38.8 us
    gather x4, local copies, waits for them, and re-layouts, one_tile(): picked = pair_blocks[windows]  32.2 us
    all_to_all x1, blocking collectives, body(): lax.all_to_all(lax.all_to_all(outgoing, 'seq', split_axis=0, concat_axis=...  22.5 us
    all_to_all x1, waiting for transfers between devices, body(): lax.all_to_all(query_sorted, 'seq', split_axis=0, concat_axis=0, tiled=True)  19.5 us
    gather x1, local copies, waits for them, and re-layouts, body(): pair_ext = padded[place_ext]  18.7 us
    scatter x1, local copies, waits for them, and re-layouts, body(): place_ext = jnp.full((ext_rows,), 3 * tok_dev, jnp.int32).at[target].set(...  17.6 us
  transfers between devices with their start and end apart: 12, of which 6 were waited for; matrix products, arithmetic and copies ran while one was open for 11% of the time, Pallas kernels for 0%

profile of v1, /device:TPU:1, one launch (start us, length us, event | category | flops | bytes accessed | tf_op | source)
XLA Modules:
  0.0 577.7 jit_solution(12577039928358637167)
XLA Ops:
  0.0 3.9 sort.17
  4.0 2.0 gather_fusion.4
  7.2 12.2 %all-to-all-start.2 = ((s32[32,1,144]{2,1,0:T(1,128)}), s32[32,1,144]{2,1,0:T(1,128)}, u32[]{:S(2)}, u32[]{:S(2)}) async-start(s32[32,1,144]{2,1,0:T(1,128)} %reshape.380), calls=%async_computation.2 | async-start | bytes 65536 | tf_op jit(solution)/shard_map/all_to_all | solution.py:94
  19.4 1.3 gather_fusion.7
  20.7 1.2 copy.154
  21.9 5.9 %all-to-all-done.2 = s32[32,1,144]{2,1,0:T(1,128)} async-done(((s32[32,1,144]{2,1,0:T(1,128)}), s32[32,1,144]{2,1,0:T(1,128)}, u32[]{:S(2)}, u32[]{:S(2)}) %all-to-all-start.2) | async-done | bytes 18464 | tf_op jit(solution)/shard_map/all_to_all | solution.py:94
  27.9 4.1 all-to-all-start.3
  32.4 1.6 pad_maximum_fusion
  34.0 2.5 gather_fusion.3
  36.8 3.3 fusion.37
  40.2 19.5 %all-to-all-done.3 = bf16[32,6,8,384]{3,2,1,0:T(8,128)(2,1)S(1)} async-done(((bf16[32,6,8,384]{3,2,1,0:T(8,128)(2,1)}), bf16[32,6,8,384]{3,2,1,0:T(8,128)(2,1)S(1)}, u32[]{:S(2)}, u32[]{:S(2)}) %all-to-all-start.3) | async-done | bytes 1179680 | tf_op jit(solution)/shard_map/all_to_all | solution.py:80
  59.7 7.0 %all-to-all-start = ((bf16[32,18,8,768]{3,2,1,0:T(8,128)(2,1)}), bf16[32,18,8,768]{3,2,1,0:T(8,128)(2,1)}, u32[]{:S(2)}, u32[]{:S(2)}) async-start(bf16[32,18,8,768]{3,2,1,0:T(8,128)(2,1)} %fusion.37), calls=%async_computation | async-start | bytes 14155776 | tf_op jit(solution)/shard_map/all_to_all | solution.py:87
  66.6 1.3 copy.125
  67.9 151.4 %all-to-all-done = bf16[32,18,8,768]{3,2,1,0:T(8,128)(2,1)} async-done(((bf16[32,18,8,768]{3,2,1,0:T(8,128)(2,1)}), bf16[32,18,8,768]{3,2,1,0:T(8,128)(2,1)}, u32[]{:S(2)}, u32[]{:S(2)}) %all-to-all-start) | async-done | bytes 7077920 | tf_op jit(solution)/shard_map/all_to_all | solution.py:87
  219.3 7.7 %all-to-all-start.4 = ((bf16[32,6,8,384]{3,0,1,2:T(8,128)(2,1)}), bf16[32,6,8,384]{3,0,1,2:T(8,128)(2,1)S(1)}, u32[]{:S(2)}, u32[]{:S(2)}) async-start(bf16[32,6,8,384]{3,0,1,2:T(8,128)(2,1)} %copy.125), calls=%async_computation.4 | async-start | bytes 2359296 | tf_op jit(solution)/shard_map/all_to_all | solution.py:79
  227.0 8.3 %copy.110 = bf16[32,18,8,768]{3,0,1,2:T(8,128)(2,1)} copy(bf16[32,18,8,768]{3,2,1,0:T(8,128)(2,1)} %all-to-all-done) | data formatting | bytes 14155776 | tf_op jit(solution)/shard_map/all_to_all | solution.py:87
  235.4 8.2 %all-to-all-done.4 = bf16[32,6,8,384]{3,0,1,2:T(8,128)(2,1)S(1)} async-done(((bf16[32,6,8,384]{3,0,1,2:T(8,128)(2,1)}), bf16[32,6,8,384]{3,0,1,2:T(8,128)(2,1)S(1)}, u32[]{:S(2)}, u32[]{:S(2)}) %all-to-all-start.4) | async-done | bytes 1179680 | tf_op jit(solution)/shard_map/all_to_all | solution.py:79
  243.5 5.6 all-to-all-start.1
  249.1 1.2 scatter_custom_fusion.2
  251.7 1.5 reduce.6
  253.8 1.6 collective-permute-start.1
  256.0 2.9 collective-permute-start.3
  259.9 2.7 collective-permute-start.5
  262.6 65.1 %collective-permute-done.1 = s32[32,18,1]{0,1,2:T(8,128)S(1)} collective-permute-done((s32[32,18,1]{0,1,2:T(8,128)S(1)}, s32[32,18,1]{0,1,2:T(8,128)S(1)}, u32[]{:S(2)}, u32[]{:S(2)}) %collective-permute-start.1) | collective-permute-done | bytes 2336 | tf_op jit(solution)/shard_map/ppermute | solution.py:27
  327.7 2.8 collective-permute-start.6
  330.6 1.5 collective-permute-done.6
  333.7 6.2 %scatter_custom_fusion.1 = s32[1536]{0:T(1024)S(1)} fusion(s32[1536]{0:T(1024)S(1)} %fusion.42, s32[1536]{0:T(1024)S(1)} %iota.29, s32[]{:T(128)} %copy.186), kind=kCustom, calls=%fused_computation.80 | custom fusion | bytes 6148 | tf_op jit(solution)/shard_map/scatter | solution.py:99
  340.0 17.6 %scatter_custom_fusion = s32[3840]{0:T(1024)S(1)} fusion(s32[4608]{0:T(1024)S(1)} %fusion.39, s32[4608]{0:T(1024)S(1)} %iota.28, s32[]{:T(128)} %constant.21.clone.1), kind=kCustom, calls=%fused_computation.72 | custom fusion | bytes 15364 | tf_op jit(solution)/shard_map/scatter | solution.py:107
  357.7 1.7 copy.126
  359.3 2.3 reshape.239
  361.6 5.3 gather_fusion.8
  367.0 3.3 reshape.370
  370.2 1.3 copy.129
  371.5 10.9 %copy.111 = bf16[32,8,18,1,768]{4,2,1,0,3:T(8,128)(2,1)} copy(bf16[32,8,18,1,768]{4,0,2,1,3:T(8,128)(2,1)} %bitcast.5) | data formatting | bytes 14155776 | tf_op jit(solution)/shard_map/all_to_all | solution.py:86
  382.4 11.5 %reshape.235 = bf16[4608,768]{1,0:T(8,128)(2,1)} reshape(bf16[32,8,18,1,768]{4,2,1,0,3:T(8,128)(2,1)} %copy.111) | data formatting | bytes 14155776 | tf_op jit(solution)/shard_map/reshape | solution.py:111
  393.9 6.4 %concatenate.28 = bf16[4609,768]{1,0:T(8,128)(2,1)} pad(bf16[4608,768]{1,0:T(8,128)(2,1)} %reshape.235, bf16[]{:T(256)} %constant.38.clone.1), padding=0_1x0_0 | pad | bytes 14157314 | tf_op jit(solution)/shard_map/concatenate | solution.py:109
  400.3 18.7 %gather_fusion.6 = bf16[3840,768]{1,0:T(8,128)(2,1)} fusion(bf16[4609,768]{1,0:T(8,128)(2,1)} %concatenate.28, s32[4096]{0:T(1024)S(1)} %pad_clamp_fusion.1), kind=kCustom, calls=%fused_computation.6 | custom fusion | bytes 11811840 | tf_op jit(solution)/shard_map/gather | solution.py:116
  419.0 13.8 %reshape.237 = bf16[10,384,2,3,128]{4,3,2,1,0:T(4,128)(2,1)} reshape(bf16[3840,768]{1,0:T(8,128)(2,1)} %gather_fusion.6) | data formatting | bytes 11796480 | tf_op jit(solution)/shard_map/reshape | solution.py:123
  432.8 72.1 %while.11 = (s32[]{:T(128)}, bf16[4,384,384]{2,1,0:T(8,128)(2,1)S(1)}, pred[4,384]{1,0:T(4,128)(4,1)S(1)}, s32[4,4]{1,0:T(4,128)S(1)}, bf16[10,384,2,3,128]{4,3,...) while((s32[]{:T(128)}, ...), condition=%wide.region_6.7_spmd.clone, body=%wide.region_3.6_spmd.clone.sunk | while | flops 925878784 | bytes 37202520 | solution.py:150
  433.7 8.1 %gather_fusion.1 = bf16[4,384,2,3,128]{4,3,2,1,0:T(4,128)(2,1)} fusion(bf16[10,384,2,3,128]{4,3,2,1,0:T(4,128)(2,1)} %get-tuple-element.211, s32[1024]{0:T(1024)S(1)} %pad_clamp_fusion.9), kind=kCustom, calls=%fused_computation.clone.clone.1 | custom fusion | bytes 4718608 | tf_op jit(solution)/shard_map/while/body/eval_jaxpr/gather | solution.py:128
  441.8 3.0 fusion.65
  445.0 2.2 fusion.66
  447.1 1.5 fusion.67
  448.7 2.0 fusion.68
  451.7 8.1 %gather_fusion.1 = bf16[4,384,2,3,128]{4,3,2,1,0:T(4,128)(2,1)} fusion(bf16[10,384,2,3,128]{4,3,2,1,0:T(4,128)(2,1)} %get-tuple-element.211, s32[1024]{0:T(1024)S(1)} %pad_clamp_fusion.9), kind=kCustom, calls=%fused_computation.clone.clone.1 | custom fusion | bytes 4718608 | tf_op jit(solution)/shard_map/while/body/eval_jaxpr/gather | solution.py:128
  459.8 3.0 fusion.65
  463.0 2.2 fusion.66
  465.1 1.5 fusion.67
  466.7 2.0 fusion.68
  469.7 8.1 %gather_fusion.1 = bf16[4,384,2,3,128]{4,3,2,1,0:T(4,128)(2,1)} fusion(bf16[10,384,2,3,128]{4,3,2,1,0:T(4,128)(2,1)} %get-tuple-element.211, s32[1024]{0:T(1024)S(1)} %pad_clamp_fusion.9), kind=kCustom, calls=%fused_computation.clone.clone.1 | custom fusion | bytes 4718608 | tf_op jit(solution)/shard_map/while/body/eval_jaxpr/gather | solution.py:128
  477.7 3.0 fusion.65
  480.9 2.2 fusion.66
  483.1 1.5 fusion.67
  484.6 2.0 fusion.68
  487.7 8.1 %gather_fusion.1 = bf16[4,384,2,3,128]{4,3,2,1,0:T(4,128)(2,1)} fusion(bf16[10,384,2,3,128]{4,3,2,1,0:T(4,128)(2,1)} %get-tuple-element.211, s32[1024]{0:T(1024)S(1)} %pad_clamp_fusion.9), kind=kCustom, calls=%fused_computation.clone.clone.1 | custom fusion | bytes 4718608 | tf_op jit(solution)/shard_map/while/body/eval_jaxpr/gather | solution.py:128
  495.7 3.0 fusion.65
  498.9 2.2 fusion.66
  501.1 1.5 fusion.67
  502.6 2.0 fusion.68
  504.9 5.3 gather_fusion.9
  510.2 2.2 reshape.242
  512.7 38.8 %all_to_all.65 = bf16[32,8,6,1,384]{4,1,3,2,0:T(8,128)(2,1)S(1)} all-to-all(bf16[32,8,6,1,384]{4,1,3,2,0:T(8,128)(2,1)S(1)} %copy.131), channel_id=1, replica_groups=mesh['seq'=32,'head'=8] {'seq'}, dimensions={0} | all-to-all | bytes 2359296 | tf_op jit(solution)/shard_map/all_to_all | solution.py:155
  551.7 22.5 %all_to_all.66 = bf16[32,8,6,1,384]{4,0,3,2,1:T(8,128)(2,1)S(1)} all-to-all(bf16[32,8,6,1,384]{4,0,3,2,1:T(8,128)(2,1)S(1)} %copy.132), channel_id=1, replica_groups=mesh['seq'=32,'head'=8] {'head'}, dimensions={1} | all-to-all | bytes 2359296 | tf_op jit(solution)/shard_map/all_to_all | solution.py:154
  575.1 2.3 gather_fusion.10
  (122 shorter events, 13.4 us)
Async XLA Ops:
  0.0 19.4 %copy-start = (bf16[192,3072]{1,0:T(8,128)(2,1)S(1)}, bf16[192,3072]{1,0:T(8,128)(2,1)}, u32[]{:S(2)}) copy-start(bf16[192,3072]{1,0:T(8,128)(2,1)} %param.8) | copy-start | bytes 3538948
  7.2 20.7 %all-to-all-start.2 = ((s32[32,1,144]{2,1,0:T(1,128)}), s32[32,1,144]{2,1,0:T(1,128)}, u32[]{:S(2)}, u32[]{:S(2)}) async-start(s32[32,1,144]{2,1,0:T(1,128)} %reshape.380), calls=%async_computation.2 | async-start | bytes 65536 | tf_op jit(solution)/shard_map/all_to_all | solution.py:94
  20.7 11.3 %copy-start.3 = (bf16[192,3072]{1,0:T(8,128)(2,1)S(1)}, bf16[192,3072]{1,0:T(8,128)(2,1)}, u32[]{:S(2)}) copy-start(bf16[192,3072]{1,0:T(8,128)(2,1)} %param.9) | copy-start | bytes 3538948
  27.9 4.3 copy-start.4
  27.9 31.8 %all-to-all-start.3 = ((bf16[32,6,8,384]{3,2,1,0:T(8,128)(2,1)}), bf16[32,6,8,384]{3,2,1,0:T(8,128)(2,1)S(1)}, u32[]{:S(2)}, u32[]{:S(2)}) async-start(bf16[32,6,8,384]{3,2,1,0:T(8,128)(2,1)} %bitcast.48), calls=%async_computation.3 | async-start | bytes 2359296 | tf_op jit(solution)/shard_map/all_to_all | solution.py:80
  59.7 159.6 %all-to-all-start = ((bf16[32,18,8,768]{3,2,1,0:T(8,128)(2,1)}), bf16[32,18,8,768]{3,2,1,0:T(8,128)(2,1)}, u32[]{:S(2)}, u32[]{:S(2)}) async-start(bf16[32,18,8,768]{3,2,1,0:T(8,128)(2,1)} %fusion.37), calls=%async_computation | async-start | bytes 14155776 | tf_op jit(solution)/shard_map/all_to_all | solution.py:87
  219.3 24.2 %all-to-all-start.4 = ((bf16[32,6,8,384]{3,0,1,2:T(8,128)(2,1)}), bf16[32,6,8,384]{3,0,1,2:T(8,128)(2,1)S(1)}, u32[]{:S(2)}, u32[]{:S(2)}) async-start(bf16[32,6,8,384]{3,0,1,2:T(8,128)(2,1)} %copy.125), calls=%async_computation.4 | async-start | bytes 2359296 | tf_op jit(solution)/shard_map/all_to_all | solution.py:79
  235.4 15.0 %copy-start.2 = (s32[128]{0:T(128)S(1)}, s32[128]{0:T(128)}, u32[]{:S(2)}) copy-start(s32[128]{0:T(128)} %param.13) | copy-start | bytes 1540
  235.4 15.8 %copy-start.5 = (s32[4,4]{1,0:T(4,128)S(1)}, s32[4,4]{1,0:T(4,128)}, u32[]{:S(2)}) copy-start(s32[4,4]{1,0:T(4,128)} %param.12) | copy-start | bytes 196
  243.5 128.0 %all-to-all-start.1 = ((bf16[32,18,8,768]{3,0,1,2:T(8,128)(2,1)}), bf16[32,18,8,768]{3,0,1,2:T(8,128)(2,1)}, u32[]{:S(2)}, u32[]{:S(2)}) async-start(bf16[32,18,8,768]{3,0,1,2:T(8,128)(2,1)} %copy.110), calls=%async_computation.1 | async-start | bytes 14155776 | tf_op jit(solution)/shard_map/all_to_all | solution.py:86
  253.6 6.3 %collective-permute-start = (s32[32,18,1]{0,1,2:T(8,128)S(1)}, s32[32,18,1]{0,1,2:T(8,128)S(1)}, u32[]{:S(2)}, u32[]{:S(2)}) collective-permute-start(s32[32,18,1]{0,1,2:T(8,128)S(1)} %copy.143), channel_id=1, source_target_pairs={{0,1},{1,0},{2,3},{3,2},{4,5},{5,4},{6,7},{7,6},{8,9},{9,8},{10,11... | collective-permute-start | bytes 6920 | tf_op jit(solution)/shard_map/ppermute | solution.py:27
  253.8 73.8 %collective-permute-start.1 = (s32[32,18,1]{0,1,2:T(8,128)S(1)}, s32[32,18,1]{0,1,2:T(8,128)S(1)}, u32[]{:S(2)}, u32[]{:S(2)}) collective-permute-start(s32[32,18,1]{0,1,2:T(8,128)S(1)} %copy.144), channel_id=1, source_target_pairs={{0,2},{1,3},{2,0},{3,1},{4,6},{5,7},{6,4},{7,5},{8,10},{9,11},{10,... | collective-permute-start | bytes 6920 | tf_op jit(solution)/shard_map/ppermute | solution.py:27
  255.5 75.0 %collective-permute-start.2 = (s32[32,18,1]{0,1,2:T(8,128)S(1)}, s32[32,18,1]{0,1,2:T(8,128)S(1)}, u32[]{:S(2)}, u32[]{:S(2)}) collective-permute-start(s32[32,18,1]{0,1,2:T(8,128)S(1)} %copy.145), channel_id=1, source_target_pairs={{0,3},{1,2},{2,1},{3,0},{4,7},{5,6},{6,5},{7,4},{8,11},{9,10},{10,... | collective-permute-start | bytes 6920 | tf_op jit(solution)/shard_map/ppermute | solution.py:27
  256.0 74.5 %collective-permute-start.3 = (s32[32,18,1]{0,1,2:T(8,128)S(1)}, s32[32,18,1]{0,1,2:T(8,128)S(1)}, u32[]{:S(2)}, u32[]{:S(2)}) collective-permute-start(s32[32,18,1]{0,1,2:T(8,128)S(1)} %copy.146), channel_id=1, source_target_pairs={{0,4},{1,5},{2,6},{3,7},{4,0},{5,1},{6,2},{7,3},{8,12},{9,13},{10,... | collective-permute-start | bytes 6920 | tf_op jit(solution)/shard_map/ppermute | solution.py:27
  259.0 71.5 %collective-permute-start.4 = (s32[32,18,1]{0,1,2:T(8,128)S(1)}, s32[32,18,1]{0,1,2:T(8,128)S(1)}, u32[]{:S(2)}, u32[]{:S(2)}) collective-permute-start(s32[32,18,1]{0,1,2:T(8,128)S(1)} %copy.147), channel_id=1, source_target_pairs={{0,5},{1,4},{2,7},{3,6},{4,1},{5,0},{6,3},{7,2},{8,13},{9,12},{10,... | collective-permute-start | bytes 6920 | tf_op jit(solution)/shard_map/ppermute | solution.py:27
  259.9 72.2 %collective-permute-start.5 = (s32[32,18,1]{0,1,2:T(8,128)S(1)}, s32[32,18,1]{0,1,2:T(8,128)S(1)}, u32[]{:S(2)}, u32[]{:S(2)}) collective-permute-start(s32[32,18,1]{0,1,2:T(8,128)S(1)} %copy.148), channel_id=1, source_target_pairs={{0,6},{1,7},{2,4},{3,5},{4,2},{5,3},{6,0},{7,1},{8,14},{9,15},{10,... | collective-permute-start | bytes 6920 | tf_op jit(solution)/shard_map/ppermute | solution.py:27
  327.7 4.4 collective-permute-start.6
  575.1 2.3 copy-start.1
